TPU v7x, 256 devices: a whole 4x4x8 slice. The times are simulated.
256 devices in a mesh: tm: 8 (over x, y_hi), rows: 32 (over z, y_lo, core).
Axes of the slice: x: 4, y: 4 (y_hi: 2, y_lo: 2; y = y_hi * 2 + y_lo), z: 8, core: 2. Of those that a mesh axis runs over, the one named last changes fastest.
Arguments:
- start_state: float32 [2, 1024, 4096], P(None, 'rows'), may hold values from -6 to 6
- guess: float32 [8, 2, 1024, 4096], P('tm', None, 'rows'), may hold values from -6 to 6
Outputs:
- corrected: float32 [8, 2, 1024, 4096], P('tm', None, 'rows')
- relaxed: float32 [8, 2, 1024, 4096], P('tm', None, 'rows')
All inputs are finite; a program needn't handle non-finite values.
Results may differ from a plain program's by a relative error of at most 0.00002.
Values sent between devices are 32-bit elements; how exact they have to be, the bound alone decides.
A program may use at most 64 MiB of HBM per device.

v0:
```python
import functools

import jax
import jax.numpy as jnp
from jax import lax
from jax.experimental import pallas as pl
from jax.experimental.pallas import tpu as pltpu
from jax.sharding import PartitionSpec as P

STEPS = 4
FINE = 0.05
COARSE = STEPS * FINE
VISCOSITY = 1.0
MESH = pl.DeviceIdType.MESH

LANES = 128
TOP = 16
FRAME = 64
HALO = 10
EDGE = 2
WIDE = 8
SPAN = WIDE + 2
GROUP = 2


def update(src, base, i, count, row, rows, size):
    lane = lax.broadcasted_iota(jnp.int32, (2, rows, LANES), 2)
    here = pl.ds(row, rows)
    left = base + jnp.maximum(i - 1, 0)
    right = base + jnp.minimum(i + 1, count - 1)
    c = src[base + i, :, here, :]
    east = pltpu.roll(jnp.where(lane == 0, src[right, :, here, :], c), LANES - 1, 2)
    west = pltpu.roll(jnp.where(lane == LANES - 1, src[left, :, here, :], c), 1, 2)
    upper = src[base + i, :, pl.ds(row + 1, rows), :]
    lower = src[base + i, :, pl.ds(row - 1, rows), :]
    u = (0.5 * size) * c[0:1]
    v = (0.5 * size) * c[1:2]
    k = size * VISCOSITY
    return (1.0 - 4.0 * k) * c + ((k - u) * east + (k + u) * west) + ((k - v) * upper + (k + v) * lower)


def kernel(
    cols, groups, strips, start_ref, guess_ref, corrected_ref, relaxed_ref,
    field, tau, w0, w1, w2, relaxed, state, mid, nxt,
    load_sem, arrive_sem, shift_sem, halo_send, halo_recv, chain_send, chain_recv, out_sem,
):
    g = lax.axis_index("tm")
    r = lax.axis_index("rows")
    x = g // 2
    up = lax.rem(r + 1, strips)
    down = lax.rem(r + strips - 1, strips)
    n_windows = cols // WIDE
    n_groups = cols // GROUP
    strip = pl.ds(TOP, 32)
    S, B, A = 0, 1, 2

    barrier = pltpu.get_barrier_semaphore()

    def greet(group, row):
        pl.semaphore_signal(barrier, inc=1, device_id=(group, row), device_id_type=MESH)

    greet(g, up)
    greet(g, down)

    @pl.when(g >= 1)
    def _():
        greet(g - 1, r)

    @pl.when(g >= 2)
    def _():
        greet(g - 2, r)
        greet(g - 2, up)
        greet(g - 2, down)

    def load(src, which, sem):
        def one(f, _):
            c = lax.rem(f + cols - 1, cols)
            pltpu.make_async_copy(
                src.at[:, :, pl.ds(pl.multiple_of(c * LANES, LANES), LANES)],
                field.at[which, f, :, strip, :],
                sem(f),
            ).start()
            return 0

        lax.fori_loop(0, cols, one, 0)

    def chunk(k):
        if k == 0:
            return 0, SPAN
        if k < n_windows - 1:
            return WIDE * k + 2, WIDE
        return WIDE * k + 2, WIDE - 2

    load(guess_ref, B, lambda f: load_sem.at[0])

    @pl.when(g == 0)
    def _():
        for k in range(n_windows):
            lo, n = chunk(k)

            def one(f, _, k=k):
                c = lax.rem(f + cols - 1, cols)
                pltpu.make_async_copy(
                    start_ref.at[:, :, pl.ds(pl.multiple_of(c * LANES, LANES), LANES)],
                    field.at[A, f, :, strip, :],
                    arrive_sem.at[k],
                ).start()
                return 0

            lax.fori_loop(lo, lo + n, one, 0)

    @pl.when(g == 1)
    def _():
        load(start_ref, S, lambda f: load_sem.at[1])

    pl.semaphore_wait(barrier, 2 + jnp.where(g < groups - 1, 1, 0) + jnp.where(g < groups - 2, 3, 0))

    def whole(which, lo, n):
        return field.at[which, pl.ds(lo, n), :, strip, :]

    def shift(k):
        lo, n = chunk(k)
        return pltpu.make_async_remote_copy(
            src_ref=whole(B, lo, n), dst_ref=whole(A, lo, n),
            send_sem=shift_sem.at[k], recv_sem=arrive_sem.at[k],
            device_id=(g + 1, r), device_id_type=MESH,
        )

    def halo(which, lo, n, slot):
        def copy(row_from, row_to, side, device):
            return pltpu.make_async_remote_copy(
                src_ref=field.at[which, pl.ds(lo, n), :, pl.ds(row_from, HALO), :],
                dst_ref=field.at[which, pl.ds(lo, n), :, pl.ds(row_to, HALO), :],
                send_sem=halo_send.at[side, slot], recv_sem=halo_recv.at[side, slot],
                device_id=(g, device), device_id_type=MESH,
            )

        return (
            copy(TOP, TOP + 32, 0, down),
            copy(TOP + 32 - HALO, TOP - HALO, 1, up),
        )

    def wrap(ref, lo, to, n):
        for i in range(n):
            ref[to + i] = ref[lo + i]

    pltpu.make_async_copy(whole(B, 0, cols), whole(B, 0, cols), load_sem.at[0]).wait()
    for copy in halo(B, 0, cols, n_windows):
        copy.start()

    @pl.when(g < groups - 1)
    def _():
        for k in range(n_windows):
            shift(k).start()

    @pl.when(g == 1)
    def _():
        pltpu.make_async_copy(whole(S, 0, cols), whole(S, 0, cols), load_sem.at[1]).wait()
        for copy in halo(S, 0, cols, n_windows + 1):
            copy.start()

    def arrived(k):
        lo, n = chunk(k)
        pltpu.make_async_copy(whole(A, lo, n), whole(A, lo, n), arrive_sem.at[k]).wait()
        for copy in halo(A, lo, n, k):
            copy.start()

    def march(src, base, which, k, steps_out):
        def run(fn):
            lax.fori_loop(0, SPAN, fn, 0, unroll=True)

        def fine(a, abase, b, row, rows):
            def one(i, _):
                b[i, :, pl.ds(row, rows), :] = update(a, abase, i, SPAN, row, rows, FINE)
                return 0

            run(one)

        fine(src, base, w0, TOP - 12, 56)
        fine(w0, 0, w1, TOP - 8, 48)
        fine(w1, 0, w0, TOP - 8, 48)
        fine(w0, 0, w2, TOP - 8, 48)
        steps_out()
        fine(w2, 0, w0, TOP - 8, 48)
        fine(w0, 0, w1, TOP - 4, 40)
        fine(w1, 0, w0, TOP - 4, 40)
        row, rows = TOP - 4, 40

        def last(i, _):
            t = update(w0, 0, i, SPAN, row, rows, FINE)
            rough = update(w2, 0, i, SPAN, row, rows, COARSE)
            tau[which, WIDE * k + i, :, pl.ds(row, rows), :] = jnp.where(which == S, t, t - rough)
            return 0

        lax.fori_loop(1, SPAN - 1, last, 0, unroll=True)

    def window(w, _):
        which = w // n_windows
        k = lax.rem(w, n_windows)

        @pl.when((which == S) & (k == 0))
        def _():
            for copy in halo(S, 0, cols, n_windows + 1):
                copy.wait_recv()
            wrap(field.at[S], 0, cols, 2)

        @pl.when((which == B) & (k == 0))
        def _():
            for copy in halo(B, 0, cols, n_windows):
                copy.wait_recv()
            wrap(field.at[B], 0, cols, 2)

        for q in range(n_windows):
            @pl.when((which == A) & (k == q))
            def _(q=q):
                if q == 0:
                    arrived(0)
                if q < n_windows - 1:
                    arrived(q + 1)
                lo, n = chunk(q)
                for copy in halo(A, lo, n, q):
                    copy.wait_recv()
                if q == n_windows - 1:
                    wrap(field.at[A], 0, cols, 2)

        def steps_out():
            @pl.when(which == A)
            def _():
                def one(i, _):
                    f = WIDE * k + i
                    relaxed[f, :, pl.ds(TOP - 8, 48), :] = w2[i, :, pl.ds(TOP - 8, 48), :]
                    pltpu.make_async_copy(
                        relaxed.at[f, :, strip, :],
                        relaxed_ref.at[:, :, pl.ds(pl.multiple_of((f - 1) * LANES, LANES), LANES)],
                        out_sem.at[0],
                    ).start()
                    return 0

                lax.fori_loop(1, SPAN - 1, one, 0)

        march(field.at[which], WIDE * k, which, k, steps_out)
        return 0

    lax.fori_loop(jnp.where(g == 1, 0, n_windows), 3 * n_windows, window, 0)

    for which in (B, A):
        tau[which, 0] = tau[which, cols]
        for i in range(3):
            tau[which, cols + 1 + i] = tau[which, 1 + i]

    @pl.when(g == 0)
    def _():
        def one(f, _):
            state[f, :, pl.ds(TOP - 8, 48), :] = relaxed[f, :, pl.ds(TOP - 8, 48), :]
            return 0

        lax.fori_loop(1, cols + 1, one, 0)

    @pl.when(g == 1)
    def _():
        def one(f, _):
            state[f, :, pl.ds(TOP - 4, 40), :] = tau[S, f, :, pl.ds(TOP - 4, 40), :]
            return 0

        lax.fori_loop(1, cols + 1, one, 0)

    @pl.when(x == 0)
    def _():
        state[0] = state[cols]
        state[cols + 1] = state[1]

    def group_in(j):
        ref = state.at[pl.ds(GROUP * j, GROUP), :, pl.ds(TOP - EDGE, 32 + 2 * EDGE), :]
        pltpu.make_async_copy(ref, ref, chain_recv.at[j]).wait()

    def put_out(p):
        c = lax.rem(p + x - 1 + cols, cols)
        pltpu.make_async_copy(
            state.at[p, :, strip, :],
            corrected_ref.at[:, :, pl.ds(pl.multiple_of(c * LANES, LANES), LANES)],
            out_sem.at[1],
        ).start()

    def group_out(j):
        def copy(row_from, n, row_to, device):
            return pltpu.make_async_remote_copy(
                src_ref=nxt.at[pl.ds(GROUP * j, GROUP), :, pl.ds(row_from, n), :],
                dst_ref=state.at[pl.ds(GROUP * j, GROUP), :, pl.ds(row_to, n), :],
                send_sem=chain_send.at[j], recv_sem=chain_recv.at[j],
                device_id=(g + 2, device), device_id_type=MESH,
            )

        copy(TOP, EDGE, TOP + 32, down).start()
        copy(TOP + 32 - EDGE, EDGE, TOP - EDGE, up).start()
        copy(TOP, 32, TOP, r).start()

    def chain(j, _):
        @pl.when(x > 0)
        def _():
            @pl.when(j == 0)
            def _():
                group_in(0)
                put_out(0)
                put_out(1)
                for i in range(2):
                    state[cols + i] = state[i]

            @pl.when(j < n_groups - 1)
            def _():
                group_in(j + 1)
                put_out(GROUP * (j + 1))
                put_out(GROUP * (j + 1) + 1)

        @pl.when(x == 0)
        def _():
            put_out(GROUP * j + 1)
            put_out(GROUP * j + 2)

        @pl.when(g < groups - 2)
        def _():
            base = GROUP * j

            def rough(i, _):
                rows = pl.ds(TOP - 4, 40)
                mid[i, :, rows, :] = update(state, base, i, GROUP + 2, TOP - 4, 40, COARSE) + tau[A, base + x + i, :, rows, :]
                return 0

            lax.fori_loop(0, GROUP + 2, rough, 0, unroll=True)

            def rough2(i, _):
                nxt[base + i, :, strip, :] = update(mid, 0, i + 1, GROUP + 2, TOP, 32, COARSE) + tau[B, base + x + 1 + i, :, strip, :]
                return 0

            lax.fori_loop(0, GROUP, rough2, 0, unroll=True)
            group_out(j)

        return 0

    lax.fori_loop(0, n_groups, chain, 0)

    for copy in halo(B, 0, cols, n_windows):
        copy.wait_send()
    for k in range(n_windows):
        lo, n = chunk(k)
        for copy in halo(A, lo, n, k):
            copy.wait_send()

    @pl.when(g == 1)
    def _():
        for copy in halo(S, 0, cols, n_windows + 1):
            copy.wait_send()

    @pl.when(g < groups - 1)
    def _():
        for k in range(n_windows):
            shift(k).wait_send()

    @pl.when(g < groups - 2)
    def _():
        def one(j, _):
            ref = nxt.at[pl.ds(GROUP * j, GROUP), :, pl.ds(TOP, 32 + 2 * EDGE), :]
            pltpu.make_async_copy(ref, ref, chain_send.at[j]).wait()
            return 0

        lax.fori_loop(0, n_groups, one, 0)

    for i in range(2):
        done = relaxed.at[pl.ds(0, cols), :, strip, :]
        pltpu.make_async_copy(done, done, out_sem.at[i]).wait()


def shards(start_state, guess):
    guess = guess[0]
    _, rows, width = guess.shape
    cols = width // LANES
    strips = lax.axis_size("rows")
    groups = lax.axis_size("tm")
    out = jax.ShapeDtypeStruct(guess.shape, guess.dtype)
    n_windows = cols // WIDE
    n_groups = cols // GROUP

    def frames(*lead):
        return pltpu.VMEM((*lead, 2, FRAME, LANES), jnp.float32)

    dma = pltpu.SemaphoreType.DMA
    corrected, relaxed = pl.pallas_call(
        functools.partial(kernel, cols, groups, strips),
        out_shape=(out, out),
        in_specs=[pl.BlockSpec(memory_space=pl.ANY)] * 2,
        out_specs=(pl.BlockSpec(memory_space=pl.ANY),) * 2,
        scratch_shapes=[
            frames(3, cols + 2), frames(3, cols + 4),
            frames(SPAN), frames(SPAN), frames(SPAN),
            frames(cols + 2), frames(cols + 2), frames(GROUP + 2), frames(cols),
            dma((2,)), dma((n_windows,)), dma((n_windows,)),
            dma((2, n_windows + 2)), dma((2, n_windows + 2)),
            dma((n_groups,)), dma((n_groups,)), dma((2,)),
        ],
        compiler_params=pltpu.CompilerParams(
            collective_id=0, has_side_effects=True, vmem_limit_bytes=48 * 2**20
        ),
    )(start_state, guess)
    return corrected[None], relaxed[None]


def solution(mesh):
    return jax.shard_map(
        shards,
        mesh=mesh,
        in_specs=(P(None, "rows", None), P("tm", None, "rows", None)),
        out_specs=(P("tm", None, "rows", None), P("tm", None, "rows", None)),
        check_vma=False,
    )
```

profile of v0, /device:TPU:22, one launch (start us, length us, event | category | flops | bytes accessed | tf_op | source)
XLA Modules:
  0.0 100.0 jit_solution(4694813472389233451)
XLA Ops:
  0.6 0.0 copy-start
  0.6 1.2 %copy-done = f32[2,32,4096]{2,1,0:T(8,128)S(1)} copy-done((f32[2,32,4096]{2,1,0:T(8,128)S(1)}, f32[2,32,4096]{2,1,0:T(8,128)}, u32[]{:S(2)}) %copy-start) | copy-done | bytes 1048600
  1.9 0.0 copy-start.1
  1.9 1.2 %copy-done.1 = f32[1,2,32,4096]{3,2,1,0:T(8,128)S(1)} copy-done((f32[1,2,32,4096]{3,2,1,0:T(8,128)S(1)}, f32[1,2,32,4096]{3,2,1,0:T(8,128)}, u32[]{:S(2)}) %copy-start.1) | copy-done | bytes 1048600
  3.1 95.0 %shard_map.41 = (f32[2,32,4096]{2,1,0:T(8,128)S(1)}, f32[2,32,4096]{2,1,0:T(8,128)S(1)}) custom-call(f32[2,32,4096]{2,1,0:T(8,128)S(1)} %copy-done, f32[2,32,4096]{2,1,0:T(8,128)S(1)} %bitcast.3), custom_call_target="tpu_custom_call" | custom-call | tf_op jit(solution)/shard_map/pallas_call | solution.py:386
  98.1 1.0 copy.6
  99.0 1.0 copy.7
Async XLA Ops:
  0.6 1.2 %copy-start = (f32[2,32,4096]{2,1,0:T(8,128)S(1)}, f32[2,32,4096]{2,1,0:T(8,128)}, u32[]{:S(2)}) copy-start(f32[2,32,4096]{2,1,0:T(8,128)} %start_ref.1) | copy-start | bytes 3145732
  1.9 1.2 %copy-start.1 = (f32[1,2,32,4096]{3,2,1,0:T(8,128)S(1)}, f32[1,2,32,4096]{3,2,1,0:T(8,128)}, u32[]{:S(2)}) copy-start(f32[1,2,32,4096]{3,2,1,0:T(8,128)} %param.3) | copy-start | bytes 3145732
where the time goes:
time: 100 us
  Pallas kernels  95 us (95%)
  local copies, waits for them, and re-layouts  4.38 us (4%)
    pallas_call x1, Pallas kernels, shards(): pl.pallas_call(functools.partial(kernel, cols, groups, strips), out_shape...  95 us
    unnamed x6, local copies, waits for them, and re-layouts  4.38 us

commit v1 on v0

v1 whole, which is shorter than its diff:
```python
import functools

import jax
import jax.numpy as jnp
from jax import lax
from jax.experimental import pallas as pl
from jax.experimental.pallas import tpu as pltpu
from jax.sharding import PartitionSpec as P

STEPS = 4
FINE = 0.05
COARSE = STEPS * FINE
VISCOSITY = 1.0
MESH = pl.DeviceIdType.MESH

LANES = 128
TOP = 16
FRAME = 64
ROWS = 32
DEEP = 9
SHALLOW = 4
EDGE = 2
WIDE = 8
SPAN = WIDE + 2
GROUP = 2


def update(src, base, i, count, row, rows, size):
    lane = lax.broadcasted_iota(jnp.int32, (2, rows, LANES), 2)
    here = pl.ds(row, rows)
    left = base + jnp.maximum(i - 1, 0)
    right = base + jnp.minimum(i + 1, count - 1)
    c = src[base + i, :, here, :]
    east = pltpu.roll(jnp.where(lane == 0, src[right, :, here, :], c), LANES - 1, 2)
    west = pltpu.roll(jnp.where(lane == LANES - 1, src[left, :, here, :], c), 1, 2)
    upper = src[base + i, :, pl.ds(row + 1, rows), :]
    lower = src[base + i, :, pl.ds(row - 1, rows), :]
    u = (0.5 * size) * c[0:1]
    v = (0.5 * size) * c[1:2]
    k = size * VISCOSITY
    return (1.0 - 4.0 * k) * c + ((k - u) * east + (k + u) * west) + ((k - v) * upper + (k + v) * lower)


def kernel(
    cols, groups, strips, start_ref, guess_ref, corrected_ref, relaxed_ref,
    field, spare, tau, w0, w1, w2, relaxed, state, mid, odd_state, nxt,
    load_sem, arrive_sem, shift_sem, edge_sem, halo_send, halo_recv,
    chain_send, chain_recv, pass_send, out_sem,
):
    g = lax.axis_index("tm")
    r = lax.axis_index("rows")
    x = g // 2
    even = lax.rem(g, 2) == 0
    core = lax.rem(r, 2)
    up = lax.rem(r + 1, strips)
    down = lax.rem(r + strips - 1, strips)
    sibling = r + 1 - 2 * core
    outer = jnp.where(core == 0, down, up)
    n_windows = cols // WIDE
    n_groups = cols // GROUP
    strip = pl.ds(TOP, ROWS)
    B, A = 0, 1
    has_next = g < groups - 1
    has_far = even & (g < groups - 2)

    barrier = pltpu.get_barrier_semaphore()

    def greet(group, row):
        pl.semaphore_signal(barrier, inc=1, device_id=(group, row), device_id_type=MESH)

    greet(g, up)
    greet(g, down)

    @pl.when(g == 0)
    def _():
        greet(1, outer)

    @pl.when(g >= 1)
    def _():
        greet(g - 1, r)
        greet(g - 1, outer)

    @pl.when(even & (g >= 2))
    def _():
        greet(g - 2, r)
        greet(g - 2, up)
        greet(g - 2, down)

    def chunk(k):
        if k == 0:
            return 0, SPAN
        if k < n_windows - 1:
            return WIDE * k + 2, WIDE
        return WIDE * k + 2, WIDE - 2

    def load(src, dst, sems):
        for k in range(n_windows):
            lo, n = chunk(k)

            def one(f, _, k=k):
                c = lax.rem(f + cols - 1, cols)
                pltpu.make_async_copy(
                    src.at[:, :, pl.ds(pl.multiple_of(c * LANES, LANES), LANES)],
                    dst.at[f, :, strip, :],
                    sems.at[k],
                ).start()
                return 0

            lax.fori_loop(lo, lo + n, one, 0)

    load(guess_ref, field.at[B], load_sem.at[0])

    @pl.when(g == 0)
    def _():
        load(start_ref, field.at[A], arrive_sem)

    @pl.when(g == 1)
    def _():
        load(start_ref, spare, load_sem.at[1])

    pl.semaphore_wait(
        barrier,
        2 + jnp.where(has_next, 2, 0) + jnp.where(g == 1, 1, 0) + jnp.where(has_far, 3, 0),
    )

    def rows_of(ref, lo, n, row, count):
        return ref.at[pl.ds(lo, n), :, pl.ds(row, count), :]

    def await_bytes(ref, sem):
        pltpu.make_async_copy(ref, ref, sem).wait()

    def sides(src, dst, lo, n, depth, send, recv, group, device, side):
        row_from, row_to = ((TOP, TOP + ROWS), (TOP + ROWS - depth, TOP - depth))[side]
        return pltpu.make_async_remote_copy(
            src_ref=rows_of(src, lo, n, row_from, depth), dst_ref=rows_of(dst, lo, n, row_to, depth),
            send_sem=send, recv_sem=recv, device_id=(group, device), device_id_type=MESH,
        )

    def shift(k):
        lo, n = chunk(k)
        return pltpu.make_async_remote_copy(
            src_ref=rows_of(field.at[B], lo, n, TOP, ROWS), dst_ref=rows_of(field.at[A], lo, n, TOP, ROWS),
            send_sem=shift_sem.at[k], recv_sem=arrive_sem.at[k],
            device_id=(g + 1, r), device_id_type=MESH,
        )

    def inner(which, k, depth):
        lo, n = chunk(k)
        f = field.at[which]
        return [
            (core == 1 - side, sides(f, f, lo, n, depth, halo_send.at[which, 0, k], halo_recv.at[which, 0, k], g, sibling, side))
            for side in (0, 1)
        ]

    def outside(k):
        lo, n = chunk(k)
        f = field.at[B]
        return [
            (core == side, sides(f, f, lo, n, DEEP, halo_send.at[B, 1, k], halo_recv.at[B, 1, k], g, outer, side))
            for side in (0, 1)
        ]

    def onward(k, depth):
        lo, n = chunk(k)
        return [
            (core == side, sides(field.at[B], field.at[A], lo, n, depth, edge_sem.at[k], arrive_sem.at[k], g + 1, outer, side))
            for side in (0, 1)
        ]

    def back(k):
        lo, n = chunk(k)
        return [
            (core == side, sides(spare, field.at[A], lo, n, DEEP, edge_sem.at[n_windows + k], arrive_sem.at[k], 0, outer, side))
            for side in (0, 1)
        ]

    def each(copies, method):
        for condition, copy in copies:
            pl.when(condition)(getattr(copy, method))

    def got(which, side, k, depth):
        lo, n = chunk(k)
        await_bytes(rows_of(field.at[which], lo, n, TOP, depth), halo_recv.at[which, side, k])

    for k in range(n_windows):
        lo, n = chunk(k)
        await_bytes(rows_of(field.at[B], lo, n, TOP, ROWS), load_sem.at[0, k])

        @pl.when(has_far)
        def _(k=k):
            each(outside(k), "start")
            each(inner(B, k, DEEP), "start")

        @pl.when(has_next & even)
        def _(k=k):
            each(onward(k, SHALLOW), "start")
            shift(k).start()

        @pl.when(has_next & ~even)
        def _(k=k):
            each(onward(k, DEEP), "start")
            shift(k).start()

        @pl.when(g == 1)
        def _(k=k):
            await_bytes(rows_of(spare, lo, n, TOP, ROWS), load_sem.at[1, k])
            each(back(k), "start")

    def arrived(k):
        lo, n = chunk(k)

        @pl.when(even)
        def _():
            await_bytes(rows_of(field.at[A], lo, n, TOP, ROWS + DEEP), arrive_sem.at[k])
            each(inner(A, k, DEEP), "start")

        @pl.when(~even)
        def _():
            await_bytes(rows_of(field.at[A], lo, n, TOP, ROWS + SHALLOW), arrive_sem.at[k])
            each(inner(A, k, SHALLOW), "start")

    def wrap(ref, lo, to, n):
        for i in range(n):
            ref[to + i] = ref[lo + i]

    def march(which, k):
        src, base = field.at[which], WIDE * k

        def fine(a, abase, b, row, rows):
            def one(i, _):
                b[i, :, pl.ds(row, rows), :] = update(a, abase, i, SPAN, row, rows, FINE)
                return 0

            lax.fori_loop(0, SPAN, one, 0, unroll=True)

        fine(src, base, w0, TOP - 8, 48)
        fine(w0, 0, w1, TOP - 8, 48)
        fine(w1, 0, w0, TOP - 8, 48)
        fine(w0, 0, w2, TOP - 8, 48)

        @pl.when(which == A)
        def _():
            def one(i, _):
                f = base + i
                there = pl.ds(pl.multiple_of((f - 1) * LANES, LANES), LANES)
                relaxed[f, :, strip, :] = w2[i, :, strip, :]
                pltpu.make_async_copy(relaxed.at[f, :, strip, :], relaxed_ref.at[:, :, there], out_sem.at[0]).start()

                @pl.when(g == 0)
                def _():
                    pltpu.make_async_copy(relaxed.at[f, :, strip, :], corrected_ref.at[:, :, there], out_sem.at[1]).start()

                return 0

            lax.fori_loop(1, SPAN - 1, one, 0)

        @pl.when(even)
        def _():
            row, rows = TOP - 4, 40
            fine(w2, 0, w0, row, rows)
            fine(w0, 0, w1, row, rows)
            fine(w1, 0, w0, row, rows)

            def last(i, _):
                t = update(w0, 0, i, SPAN, row, rows, FINE)
                rough = update(w2, 0, i, SPAN, row, rows, COARSE)
                tau[which, base + i, :, pl.ds(row, rows), :] = jnp.where((g == 0) & (which == A), t, t - rough)
                return 0

            lax.fori_loop(1, SPAN - 1, last, 0, unroll=True)

    def window(w, _):
        k = w // 2
        which = lax.rem(w, 2)
        for q in range(n_windows):
            @pl.when((which == B) & (k == q) & has_far)
            def _(q=q):
                got(B, 0, q, DEEP)
                got(B, 1, q, DEEP)
                if q == n_windows - 1:
                    wrap(field.at[B], 0, cols, 2)

            @pl.when((which == A) & (k == q))
            def _(q=q):
                if q == 0:
                    arrived(0)
                if q < n_windows - 1:
                    arrived(q + 1)

                @pl.when(even)
                def _():
                    got(A, 0, q, DEEP)

                @pl.when(~even)
                def _():
                    got(A, 0, q, SHALLOW)

                if q == n_windows - 1:
                    wrap(field.at[A], 0, cols, 2)

        @pl.when((which == A) | has_far)
        def _():
            march(which, k)

        return 0

    def put_out(ref, p, offset):
        c = lax.rem(p + offset, cols)
        pltpu.make_async_copy(
            ref.at[p, :, strip, :],
            corrected_ref.at[:, :, pl.ds(pl.multiple_of(c * LANES, LANES), LANES)],
            out_sem.at[1],
        ).start()

    def group_in(j, extra):
        await_bytes(rows_of(state, GROUP * j, GROUP, TOP - extra, ROWS + 2 * extra), chain_recv.at[j])

    def group_out(j):
        def copy(row_from, n, row_to, device):
            return pltpu.make_async_remote_copy(
                src_ref=rows_of(nxt, GROUP * j, GROUP, row_from, n),
                dst_ref=rows_of(state, GROUP * j, GROUP, row_to, n),
                send_sem=chain_send.at[j], recv_sem=chain_recv.at[j],
                device_id=(g + 2, device), device_id_type=MESH,
            )

        copy(TOP, EDGE, TOP + ROWS, down).start()
        copy(TOP + ROWS - EDGE, EDGE, TOP - EDGE, up).start()
        copy(TOP, ROWS, TOP, r).start()

    def pass_on(j):
        return pltpu.make_async_remote_copy(
            src_ref=rows_of(odd_state, GROUP * j, GROUP, TOP, ROWS),
            dst_ref=rows_of(state, GROUP * j, GROUP, TOP, ROWS),
            send_sem=pass_send.at[j], recv_sem=chain_recv.at[j],
            device_id=(g + 1, r), device_id_type=MESH,
        )

    def chain(j, _):
        base = GROUP * j
        row, rows = TOP - 4, 40

        @pl.when(x > 0)
        def _():
            @pl.when(j == 0)
            def _():
                group_in(0, EDGE)
                wrap(state, 0, cols, 2)
                for i in range(GROUP):
                    put_out(state, i, x)

            @pl.when(j < n_groups - 1)
            def _():
                group_in(j + 1, EDGE)
                for i in range(GROUP):
                    put_out(state, GROUP * (j + 1) + i, x)

            def rough(i, _):
                mid[i, :, pl.ds(row, rows), :] = update(state, base, i, GROUP + 2, row, rows, COARSE) + tau[A, base + x + 1 + i, :, pl.ds(row, rows), :]
                return 0

            lax.fori_loop(0, GROUP + 2, rough, 0, unroll=True)

        @pl.when(x == 0)
        def _():
            def same(i, _):
                mid[i, :, pl.ds(row, rows), :] = tau[A, base + 1 + i, :, pl.ds(row, rows), :]
                return 0

            lax.fori_loop(0, GROUP + 2, same, 0, unroll=True)

        for i in range(GROUP):
            odd_state[base + i, :, strip, :] = mid[1 + i, :, strip, :]

        @pl.when(has_far)
        def _():
            def rough(i, _):
                nxt[base + i, :, strip, :] = update(mid, 0, i + 1, GROUP + 2, TOP, ROWS, COARSE) + tau[B, base + x + 2 + i, :, strip, :]
                return 0

            lax.fori_loop(0, GROUP, rough, 0, unroll=True)
            group_out(j)

        pass_on(j).start()
        return 0

    ahead = WIDE // GROUP

    def rounds(k, _):
        @pl.when(k < n_windows)
        def _():
            lax.fori_loop(2 * k, 2 * k + 2, window, 0)

        @pl.when(k == n_windows)
        def _():
            for which in (B, A):
                for i in range(5):
                    tau[which, cols + 1 + i] = tau[which, 1 + i]

        @pl.when(even)
        def _():
            first = jnp.maximum(ahead * (k - 1 - x) + 2, 0)
            stop = jnp.maximum(ahead * (k - x) + 2, 0)
            lax.fori_loop(first, jnp.where(k == n_windows, n_groups, stop), chain, 0)

        return 0

    lax.fori_loop(0, n_windows + 1, rounds, 0)

    @pl.when(~even)
    def _():
        def one(j, _):
            group_in(j, 0)
            for i in range(GROUP):
                put_out(state, GROUP * j + i, x + 1)
            return 0

        lax.fori_loop(0, n_groups, one, 0)

    for k in range(n_windows):
        @pl.when(has_far)
        def _(k=k):
            each(outside(k), "wait_send")
            each(inner(B, k, DEEP), "wait_send")

        @pl.when(has_next & even)
        def _(k=k):
            each(onward(k, SHALLOW), "wait_send")

        @pl.when(has_next & ~even)
        def _(k=k):
            each(onward(k, DEEP), "wait_send")

        @pl.when(has_next)
        def _(k=k):
            shift(k).wait_send()

        @pl.when(even)
        def _(k=k):
            each(inner(A, k, DEEP), "wait_send")

        @pl.when(~even)
        def _(k=k):
            each(inner(A, k, SHALLOW), "wait_send")

        @pl.when(g == 1)
        def _(k=k):
            each(back(k), "wait_send")

    @pl.when(even)
    def _():
        def one(j, _):
            pass_on(j).wait_send()

            @pl.when(has_far)
            def _():
                await_bytes(rows_of(nxt, GROUP * j, GROUP, TOP, ROWS + 2 * EDGE), chain_send.at[j])

            return 0

        lax.fori_loop(0, n_groups, one, 0)

    for i in range(2):
        await_bytes(rows_of(relaxed, 1, cols, TOP, ROWS), out_sem.at[i])


def shards(start_state, guess):
    guess = guess[0]
    width = guess.shape[2]
    cols = width // LANES
    strips = lax.axis_size("rows")
    groups = lax.axis_size("tm")
    out = jax.ShapeDtypeStruct(guess.shape, guess.dtype)
    n_windows = cols // WIDE
    n_groups = cols // GROUP

    def frames(*lead):
        return pltpu.VMEM((*lead, 2, FRAME, LANES), jnp.float32)

    dma = pltpu.SemaphoreType.DMA
    corrected, relaxed = pl.pallas_call(
        functools.partial(kernel, cols, groups, strips),
        out_shape=(out, out),
        in_specs=[pl.BlockSpec(memory_space=pl.ANY)] * 2,
        out_specs=(pl.BlockSpec(memory_space=pl.ANY),) * 2,
        scratch_shapes=[
            frames(2, cols + 2), frames(cols), frames(2, cols + 6),
            frames(SPAN), frames(SPAN), frames(SPAN),
            frames(cols + 1), frames(cols + 2), frames(GROUP + 2), frames(cols), frames(cols),
            dma((2, n_windows)), dma((n_windows,)), dma((n_windows,)), dma((2 * n_windows,)),
            dma((2, 2, n_windows)), dma((2, 2, n_windows)),
            dma((n_groups,)), dma((n_groups,)), dma((n_groups,)), dma((2,)),
        ],
        compiler_params=pltpu.CompilerParams(
            collective_id=0, has_side_effects=True, vmem_limit_bytes=62 * 2**20
        ),
    )(start_state, guess)
    return corrected[None], relaxed[None]


def solution(mesh):
    return jax.shard_map(
        shards,
        mesh=mesh,
        in_specs=(P(None, "rows", None), P("tm", None, "rows", None)),
        out_specs=(P("tm", None, "rows", None), P("tm", None, "rows", None)),
        check_vma=False,
    )
```

time: 100 us -> 87.5 us (0.88)
  the two profiles are of different devices: /device:TPU:22 before, /device:TPU:126 now
where the time goes in v1:
time: 87.5 us; the launch traced here: 87.3 us
  Pallas kernels  83.3 us (95%)
  local copies, waits for them, and re-layouts  3.33 us (4%)
    pallas_call x1, Pallas kernels, shards(): pl.pallas_call(functools.partial(kernel, cols, groups, strips), out_shape...  83.3 us
    unnamed x4, local copies, waits for them, and re-layouts  3.33 us

profile of v1, /device:TPU:126, one launch (start us, length us, event | category | flops | bytes accessed | tf_op | source)
XLA Modules:
  0.0 87.3 jit_solution(12905944564297439595)
XLA Ops:
  0.6 83.3 %shard_map.41 = (f32[2,32,4096]{2,1,0:T(8,128)}, f32[2,32,4096]{2,1,0:T(8,128)}) custom-call(f32[2,32,4096]{2,1,0:T(8,128)} %start_ref.1, f32[2,32,4096]{2,1,0:T(8,128)} %bitcast.3), custom_call_target="tpu_custom_call" | custom-call | tf_op jit(solution)/shard_map/pallas_call | solution.py:481
  83.9 0.0 copy-start
  83.9 2.4 %copy.6 = f32[1,2,32,4096]{3,2,1,0:T(8,128)} copy(f32[1,2,32,4096]{3,2,1,0:T(8,128)} %bitcast.5) | data formatting | bytes 2097152
  86.3 0.0 copy-done
  86.3 1.0 %copy.7 = f32[1,2,32,4096]{3,2,1,0:T(8,128)} copy(f32[1,2,32,4096]{3,2,1,0:T(8,128)S(1)} %bitcast.4) | data formatting | bytes 2097152
Async XLA Ops:
  83.9 2.4 %copy-start = (f32[2,32,4096]{2,1,0:T(8,128)S(1)}, f32[2,32,4096]{2,1,0:T(8,128)}, u32[]{:S(2)}) copy-start(f32[2,32,4096]{2,1,0:T(8,128)} %get-tuple-element.5) | copy-start | bytes 3145732

commit v2 on v1

--- a/solution.py
+++ b/solution.py
@@ -18,9 +18,10 @@
 FRAME = 64
 ROWS = 32
 DEEP = 9
+OWN = 8
 SHALLOW = 4
 EDGE = 2
-WIDE = 8
+WIDE = 4
 SPAN = WIDE + 2
 GROUP = 2
 
@@ -156,7 +157,7 @@
         lo, n = chunk(k)
         f = field.at[B]
         return [
-            (core == side, sides(f, f, lo, n, DEEP, halo_send.at[B, 1, k], halo_recv.at[B, 1, k], g, outer, side))
+            (core == side, sides(f, f, lo, n, OWN, halo_send.at[B, 1, k], halo_recv.at[B, 1, k], g, outer, side))
             for side in (0, 1)
         ]
 
@@ -182,6 +183,13 @@
         lo, n = chunk(k)
         await_bytes(rows_of(field.at[which], lo, n, TOP, depth), halo_recv.at[which, side, k])
 
+    @pl.when(g == 1)
+    def _():
+        for k in range(n_windows):
+            lo, n = chunk(k)
+            await_bytes(rows_of(spare, lo, n, TOP, ROWS), load_sem.at[1, k])
+            each(back(k), "start")
+
     for k in range(n_windows):
         lo, n = chunk(k)
         await_bytes(rows_of(field.at[B], lo, n, TOP, ROWS), load_sem.at[0, k])
@@ -189,7 +197,7 @@
         @pl.when(has_far)
         def _(k=k):
             each(outside(k), "start")
-            each(inner(B, k, DEEP), "start")
+            each(inner(B, k, OWN), "start")
 
         @pl.when(has_next & even)
         def _(k=k):
@@ -200,11 +208,6 @@
         def _(k=k):
             each(onward(k, DEEP), "start")
             shift(k).start()
-
-        @pl.when(g == 1)
-        def _(k=k):
-            await_bytes(rows_of(spare, lo, n, TOP, ROWS), load_sem.at[1, k])
-            each(back(k), "start")
 
     def arrived(k):
         lo, n = chunk(k)
@@ -223,36 +226,75 @@
         for i in range(n):
             ref[to + i] = ref[lo + i]
 
-    def march(which, k):
-        src, base = field.at[which], WIDE * k
-
-        def fine(a, abase, b, row, rows):
-            def one(i, _):
-                b[i, :, pl.ds(row, rows), :] = update(a, abase, i, SPAN, row, rows, FINE)
-                return 0
-
-            lax.fori_loop(0, SPAN, one, 0, unroll=True)
-
-        fine(src, base, w0, TOP - 8, 48)
+    def fine(a, abase, b, row, rows):
+        def one(i, _):
+            b[i, :, pl.ds(row, rows), :] = update(a, abase, i, SPAN, row, rows, FINE)
+            return 0
+
+        lax.fori_loop(0, SPAN, one, 0, unroll=True)
+
+    def excess(which, k, row, rows, rough):
+        def one(i, _):
+            t = update(w0, 0, i, SPAN, row, rows, FINE)
+            if rough:
+                t = t - update(w2, 0, i, SPAN, row, rows, COARSE)
+            tau[which, WIDE * k + i, :, pl.ds(row, rows), :] = t
+            return 0
+
+        lax.fori_loop(1, SPAN - 1, one, 0, unroll=True)
+
+    def march_own(k):
+        for q in range(n_windows):
+            @pl.when(k == q)
+            def _(q=q):
+                got(B, 0, q, OWN)
+                got(B, 1, q, OWN)
+                if q == n_windows - 1:
+                    wrap(field.at[B], 0, cols, 2)
+
+        fine(field.at[B], WIDE * k, w0, TOP - 8, 48)
+        fine(w0, 0, w1, TOP - 8, 48)
+        fine(w1, 0, w0, TOP - 8, 48)
+        fine(w0, 0, w2, TOP - 4, 40)
+        fine(w2, 0, w0, TOP - 4, 40)
+        fine(w0, 0, w1, TOP - 4, 40)
+        fine(w1, 0, w0, TOP - 4, 40)
+        excess(B, k, TOP, ROWS, True)
+
+    def march_prior(k):
+        for q in range(n_windows):
+            @pl.when(k == q)
+            def _(q=q):
+                @pl.when(even)
+                def _():
+                    got(A, 0, q, DEEP)
+
+                @pl.when(~even)
+                def _():
+                    got(A, 0, q, SHALLOW)
+
+                if q == n_windows - 1:
+                    wrap(field.at[A], 0, cols, 2)
+
+        base = WIDE * k
+        fine(field.at[A], base, w0, TOP - 8, 48)
         fine(w0, 0, w1, TOP - 8, 48)
         fine(w1, 0, w0, TOP - 8, 48)
         fine(w0, 0, w2, TOP - 8, 48)
 
-        @pl.when(which == A)
-        def _():
-            def one(i, _):
-                f = base + i
-                there = pl.ds(pl.multiple_of((f - 1) * LANES, LANES), LANES)
-                relaxed[f, :, strip, :] = w2[i, :, strip, :]
-                pltpu.make_async_copy(relaxed.at[f, :, strip, :], relaxed_ref.at[:, :, there], out_sem.at[0]).start()
-
-                @pl.when(g == 0)
-                def _():
-                    pltpu.make_async_copy(relaxed.at[f, :, strip, :], corrected_ref.at[:, :, there], out_sem.at[1]).start()
-
-                return 0
-
-            lax.fori_loop(1, SPAN - 1, one, 0)
+        def put(i, _):
+            f = base + i
+            there = pl.ds(pl.multiple_of((f - 1) * LANES, LANES), LANES)
+            relaxed[f, :, strip, :] = w2[i, :, strip, :]
+            pltpu.make_async_copy(relaxed.at[f, :, strip, :], relaxed_ref.at[:, :, there], out_sem.at[0]).start()
+
+            @pl.when(g == 0)
+            def _():
+                pltpu.make_async_copy(relaxed.at[f, :, strip, :], corrected_ref.at[:, :, there], out_sem.at[1]).start()
+
+            return 0
+
+        lax.fori_loop(1, SPAN - 1, put, 0)
 
         @pl.when(even)
         def _():
@@ -261,48 +303,13 @@
             fine(w0, 0, w1, row, rows)
             fine(w1, 0, w0, row, rows)
 
-            def last(i, _):
-                t = update(w0, 0, i, SPAN, row, rows, FINE)
-                rough = update(w2, 0, i, SPAN, row, rows, COARSE)
-                tau[which, base + i, :, pl.ds(row, rows), :] = jnp.where((g == 0) & (which == A), t, t - rough)
-                return 0
-
-            lax.fori_loop(1, SPAN - 1, last, 0, unroll=True)
-
-    def window(w, _):
-        k = w // 2
-        which = lax.rem(w, 2)
-        for q in range(n_windows):
-            @pl.when((which == B) & (k == q) & has_far)
-            def _(q=q):
-                got(B, 0, q, DEEP)
-                got(B, 1, q, DEEP)
-                if q == n_windows - 1:
-                    wrap(field.at[B], 0, cols, 2)
-
-            @pl.when((which == A) & (k == q))
-            def _(q=q):
-                if q == 0:
-                    arrived(0)
-                if q < n_windows - 1:
-                    arrived(q + 1)
-
-                @pl.when(even)
-                def _():
-                    got(A, 0, q, DEEP)
-
-                @pl.when(~even)
-                def _():
-                    got(A, 0, q, SHALLOW)
-
-                if q == n_windows - 1:
-                    wrap(field.at[A], 0, cols, 2)
-
-        @pl.when((which == A) | has_far)
-        def _():
-            march(which, k)
-
-        return 0
+            @pl.when(g == 0)
+            def _():
+                excess(A, k, row, rows, False)
+
+            @pl.when(g > 0)
+            def _():
+                excess(A, k, row, rows, True)
 
     def put_out(ref, p, offset):
         c = lax.rem(p + offset, cols)
@@ -328,9 +335,9 @@
         copy(TOP + ROWS - EDGE, EDGE, TOP - EDGE, up).start()
         copy(TOP, ROWS, TOP, r).start()
 
-    def pass_on(j):
+    def pass_on(j, src, first):
         return pltpu.make_async_remote_copy(
-            src_ref=rows_of(odd_state, GROUP * j, GROUP, TOP, ROWS),
+            src_ref=rows_of(src, first, GROUP, TOP, ROWS),
             dst_ref=rows_of(state, GROUP * j, GROUP, TOP, ROWS),
             send_sem=pass_send.at[j], recv_sem=chain_recv.at[j],
             device_id=(g + 1, r), device_id_type=MESH,
@@ -340,6 +347,14 @@
         base = GROUP * j
         row, rows = TOP - 4, 40
 
+        def onward_state(src, first):
+            def rough(i, _):
+                nxt[base + i, :, strip, :] = update(src, first, i + 1, GROUP + 2, TOP, ROWS, COARSE) + tau[B, base + x + 2 + i, :, strip, :]
+                return 0
+
+            lax.fori_loop(0, GROUP, rough, 0, unroll=True)
+            group_out(j)
+
         @pl.when(x > 0)
         def _():
             @pl.when(j == 0)
@@ -361,35 +376,38 @@
 
             lax.fori_loop(0, GROUP + 2, rough, 0, unroll=True)
 
+            @pl.when(has_far)
+            def _():
+                onward_state(mid, 0)
+
+            for i in range(GROUP):
+                odd_state[base + i, :, strip, :] = mid[1 + i, :, strip, :]
+            pass_on(j, odd_state, base).start()
+
         @pl.when(x == 0)
         def _():
-            def same(i, _):
-                mid[i, :, pl.ds(row, rows), :] = tau[A, base + 1 + i, :, pl.ds(row, rows), :]
-                return 0
-
-            lax.fori_loop(0, GROUP + 2, same, 0, unroll=True)
-
-        for i in range(GROUP):
-            odd_state[base + i, :, strip, :] = mid[1 + i, :, strip, :]
-
-        @pl.when(has_far)
-        def _():
-            def rough(i, _):
-                nxt[base + i, :, strip, :] = update(mid, 0, i + 1, GROUP + 2, TOP, ROWS, COARSE) + tau[B, base + x + 2 + i, :, strip, :]
-                return 0
-
-            lax.fori_loop(0, GROUP, rough, 0, unroll=True)
-            group_out(j)
-
-        pass_on(j).start()
+            onward_state(tau.at[A], base + 1)
+            pass_on(j, tau.at[A], base + 2).start()
+
         return 0
 
     ahead = WIDE // GROUP
+    lead = jnp.where(x == 0, 0, 2)
 
     def rounds(k, _):
-        @pl.when(k < n_windows)
-        def _():
-            lax.fori_loop(2 * k, 2 * k + 2, window, 0)
+        now = (k >= 0) & (k < n_windows)
+        for q in range(n_windows):
+            @pl.when(k == q)
+            def _(q=q):
+                arrived(q)
+
+        @pl.when(has_far & (k + lead < n_windows))
+        def _():
+            march_own(k + lead)
+
+        @pl.when(now)
+        def _():
+            march_prior(k)
 
         @pl.when(k == n_windows)
         def _():
@@ -399,13 +417,13 @@
 
         @pl.when(even)
         def _():
-            first = jnp.maximum(ahead * (k - 1 - x) + 2, 0)
-            stop = jnp.maximum(ahead * (k - x) + 2, 0)
+            first = jnp.maximum(ahead * (k - 1) + 1 - x, 0)
+            stop = jnp.maximum(ahead * k + 1 - x, 0)
             lax.fori_loop(first, jnp.where(k == n_windows, n_groups, stop), chain, 0)
 
         return 0
 
-    lax.fori_loop(0, n_windows + 1, rounds, 0)
+    lax.fori_loop(-lead, n_windows + 1, rounds, 0)
 
     @pl.when(~even)
     def _():
@@ -421,7 +439,7 @@
         @pl.when(has_far)
         def _(k=k):
             each(outside(k), "wait_send")
-            each(inner(B, k, DEEP), "wait_send")
+            each(inner(B, k, OWN), "wait_send")
 
         @pl.when(has_next & even)
         def _(k=k):
@@ -450,7 +468,7 @@
     @pl.when(even)
     def _():
         def one(j, _):
-            pass_on(j).wait_send()
+            pass_on(j, odd_state, 0).wait_send()
 
             @pl.when(has_far)
             def _():
@@ -492,7 +510,7 @@
             dma((n_groups,)), dma((n_groups,)), dma((n_groups,)), dma((2,)),
         ],
         compiler_params=pltpu.CompilerParams(
-            collective_id=0, has_side_effects=True, vmem_limit_bytes=62 * 2**20
+            collective_id=0, has_side_effects=True, vmem_limit_bytes=61 * 2**20
         ),
     )(start_state, guess)
     return corrected[None], relaxed[None]

time: 87.5 us -> 73.8 us (0.84)
  the two profiles are of different devices: /device:TPU:126 before, /device:TPU:22 now
where the time goes in v2:
time: 73.8 us; the launch traced here: 73.6 us
  Pallas kernels  69.6 us (94%)
  local copies, waits for them, and re-layouts  3.33 us (5%)
    pallas_call x1, Pallas kernels, shards(): pl.pallas_call(functools.partial(kernel, cols, groups, strips), out_shape...  69.6 us
    unnamed x4, local copies, waits for them, and re-layouts  3.33 us

profile of v2, /device:TPU:22, one launch (start us, length us, event | category | flops | bytes accessed | tf_op | source)
XLA Modules:
  0.0 73.6 jit_solution(15503018809165058062)
XLA Ops:
  0.6 69.6 %shard_map.41 = (f32[2,32,4096]{2,1,0:T(8,128)}, f32[2,32,4096]{2,1,0:T(8,128)}) custom-call(f32[2,32,4096]{2,1,0:T(8,128)} %start_ref.1, f32[2,32,4096]{2,1,0:T(8,128)} %bitcast.3), custom_call_target="tpu_custom_call" | custom-call | tf_op jit(solution)/shard_map/pallas_call | solution.py:499
  70.2 0.0 copy-start
  70.2 2.4 %copy.6 = f32[1,2,32,4096]{3,2,1,0:T(8,128)} copy(f32[1,2,32,4096]{3,2,1,0:T(8,128)} %bitcast.5) | data formatting | bytes 2097152
  72.6 0.0 copy-done
  72.6 1.0 %copy.7 = f32[1,2,32,4096]{3,2,1,0:T(8,128)} copy(f32[1,2,32,4096]{3,2,1,0:T(8,128)S(1)} %bitcast.4) | data formatting | bytes 2097152
Async XLA Ops:
  70.2 2.4 %copy-start = (f32[2,32,4096]{2,1,0:T(8,128)S(1)}, f32[2,32,4096]{2,1,0:T(8,128)}, u32[]{:S(2)}) copy-start(f32[2,32,4096]{2,1,0:T(8,128)} %get-tuple-element.5) | copy-start | bytes 3145732

commit v3 on v2

--- a/solution.py
+++ b/solution.py
@@ -23,6 +23,7 @@
 EDGE = 2
 WIDE = 4
 SPAN = WIDE + 2
+BROAD = 4
 GROUP = 2
 
 
@@ -44,7 +45,7 @@
 
 def kernel(
     cols, groups, strips, start_ref, guess_ref, corrected_ref, relaxed_ref,
-    field, spare, tau, w0, w1, w2, relaxed, state, mid, odd_state, nxt,
+    field, spare, tau, steps, relaxed, state, mid, odd_state, nxt,
     load_sem, arrive_sem, shift_sem, edge_sem, halo_send, halo_recv,
     chain_send, chain_recv, pass_send, out_sem,
 ):
@@ -153,11 +154,11 @@
             for side in (0, 1)
         ]
 
-    def outside(k):
-        lo, n = chunk(k)
-        f = field.at[B]
+    def outside(which, k, depth):
+        lo, n = chunk(k)
+        f = field.at[which]
         return [
-            (core == side, sides(f, f, lo, n, OWN, halo_send.at[B, 1, k], halo_recv.at[B, 1, k], g, outer, side))
+            (core == side, sides(f, f, lo, n, depth, halo_send.at[which, 1, k], halo_recv.at[which, 1, k], g, outer, side))
             for side in (0, 1)
         ]
 
@@ -196,7 +197,7 @@
 
         @pl.when(has_far)
         def _(k=k):
-            each(outside(k), "start")
+            each(outside(B, k, OWN), "start")
             each(inner(B, k, OWN), "start")
 
         @pl.when(has_next & even)
@@ -226,40 +227,54 @@
         for i in range(n):
             ref[to + i] = ref[lo + i]
 
-    def fine(a, abase, b, row, rows):
+    def fine(src, dst, base, wide, row, rows):
         def one(i, _):
-            b[i, :, pl.ds(row, rows), :] = update(a, abase, i, SPAN, row, rows, FINE)
+            dst[base + i, :, pl.ds(row, rows), :] = update(src, base, i, wide + 2, row, rows, FINE)
             return 0
 
-        lax.fori_loop(0, SPAN, one, 0, unroll=True)
-
-    def excess(which, k, row, rows, rough):
+        lax.fori_loop(1, wide + 2, one, 0, unroll=True)
+
+    def excess(w, out, base, wide, row, rows, rough):
         def one(i, _):
-            t = update(w0, 0, i, SPAN, row, rows, FINE)
+            t = update(w.at[6], base, i, wide + 2, row, rows, FINE)
             if rough:
-                t = t - update(w2, 0, i, SPAN, row, rows, COARSE)
-            tau[which, WIDE * k + i, :, pl.ds(row, rows), :] = t
+                t = t - update(w.at[STEPS - 1], base, i, wide + 2, row, rows, COARSE)
+            out[base + i, :, pl.ds(row, rows), :] = t
             return 0
 
-        lax.fori_loop(1, SPAN - 1, one, 0, unroll=True)
+        lax.fori_loop(1, wide + 2, one, 0, unroll=True)
+
+    def mend(ref, row, rows):
+        lane = lax.broadcasted_iota(jnp.int32, (2, rows, LANES), 2)
+        here = pl.ds(row, rows)
+        ref[1, :, here, :] = jnp.where(lane < LANES // 2, ref[cols + 1, :, here, :], ref[1, :, here, :])
 
     def march_own(k):
-        for q in range(n_windows):
+        for q in range(cols // BROAD):
             @pl.when(k == q)
             def _(q=q):
-                got(B, 0, q, OWN)
-                got(B, 1, q, OWN)
-                if q == n_windows - 1:
+                for p in range(q * BROAD // WIDE, (q + 1) * BROAD // WIDE):
+                    got(B, 0, p, OWN)
+                    got(B, 1, p, OWN)
+                if q == cols // BROAD - 1:
                     wrap(field.at[B], 0, cols, 2)
 
-        fine(field.at[B], WIDE * k, w0, TOP - 8, 48)
-        fine(w0, 0, w1, TOP - 8, 48)
-        fine(w1, 0, w0, TOP - 8, 48)
-        fine(w0, 0, w2, TOP - 4, 40)
-        fine(w2, 0, w0, TOP - 4, 40)
-        fine(w0, 0, w1, TOP - 4, 40)
-        fine(w1, 0, w0, TOP - 4, 40)
-        excess(B, k, TOP, ROWS, True)
+        w = steps.at[B]
+        base = BROAD * k
+        fine(field.at[B], w.at[0], base, BROAD, TOP - 8, 48)
+        for n in range(1, 7):
+            row, rows = (TOP - 8, 48) if n < 3 else (TOP - 4, 40)
+            fine(w.at[n - 1], w.at[n], base, BROAD, row, rows)
+        excess(w, tau.at[B], base, BROAD, TOP, ROWS, True)
+
+    def put(f):
+        there = pl.ds(pl.multiple_of((f - 1) * LANES, LANES), LANES)
+        relaxed[f, :, strip, :] = steps[A, STEPS - 1, f, :, strip, :]
+        pltpu.make_async_copy(relaxed.at[f, :, strip, :], relaxed_ref.at[:, :, there], out_sem.at[0]).start()
+
+        @pl.when(g == 0)
+        def _():
+            pltpu.make_async_copy(relaxed.at[f, :, strip, :], corrected_ref.at[:, :, there], out_sem.at[1]).start()
 
     def march_prior(k):
         for q in range(n_windows):
@@ -277,39 +292,35 @@
                     wrap(field.at[A], 0, cols, 2)
 
         base = WIDE * k
-        fine(field.at[A], base, w0, TOP - 8, 48)
-        fine(w0, 0, w1, TOP - 8, 48)
-        fine(w1, 0, w0, TOP - 8, 48)
-        fine(w0, 0, w2, TOP - 8, 48)
-
-        def put(i, _):
-            f = base + i
-            there = pl.ds(pl.multiple_of((f - 1) * LANES, LANES), LANES)
-            relaxed[f, :, strip, :] = w2[i, :, strip, :]
-            pltpu.make_async_copy(relaxed.at[f, :, strip, :], relaxed_ref.at[:, :, there], out_sem.at[0]).start()
+        w = steps.at[A]
+        row, rows = TOP - 4, 40
+        fine(field.at[A], w.at[0], base, WIDE, TOP - 8, 48)
+        for n in range(1, STEPS):
+            fine(w.at[n - 1], w.at[n], base, WIDE, TOP - 8, 48)
+
+        def one(f, _):
+            put(f)
+            return 0
+
+        lax.fori_loop(jnp.maximum(base + 1, 2), base + WIDE + 1, one, 0)
+
+        @pl.when(k == n_windows - 1)
+        def _():
+            mend(steps.at[A, STEPS - 1], TOP, ROWS)
+            put(1)
+
+        @pl.when(even)
+        def _():
+            for n in range(STEPS, 7):
+                fine(w.at[n - 1], w.at[n], base, WIDE, row, rows)
 
             @pl.when(g == 0)
             def _():
-                pltpu.make_async_copy(relaxed.at[f, :, strip, :], corrected_ref.at[:, :, there], out_sem.at[1]).start()
-
-            return 0
-
-        lax.fori_loop(1, SPAN - 1, put, 0)
-
-        @pl.when(even)
-        def _():
-            row, rows = TOP - 4, 40
-            fine(w2, 0, w0, row, rows)
-            fine(w0, 0, w1, row, rows)
-            fine(w1, 0, w0, row, rows)
-
-            @pl.when(g == 0)
-            def _():
-                excess(A, k, row, rows, False)
+                excess(w, tau.at[A], base, WIDE, row, rows, False)
 
             @pl.when(g > 0)
             def _():
-                excess(A, k, row, rows, True)
+                excess(w, tau.at[A], base, WIDE, row, rows, True)
 
     def put_out(ref, p, offset):
         c = lax.rem(p + offset, cols)
@@ -392,28 +403,41 @@
         return 0
 
     ahead = WIDE // GROUP
-    lead = jnp.where(x == 0, 0, 2)
+    lead = jnp.where(x == 0, 0, 1)
+    per = BROAD // WIDE
 
     def rounds(k, _):
         now = (k >= 0) & (k < n_windows)
         for q in range(n_windows):
-            @pl.when(k == q)
+            @pl.when((k == q) & ((x == 0) | (q == 0)))
             def _(q=q):
                 arrived(q)
 
-        @pl.when(has_far & (k + lead < n_windows))
-        def _():
-            march_own(k + lead)
+        @pl.when(has_far & (k + lead < n_windows) & (lax.rem(k + lead, per) == 0))
+        def _():
+            march_own((k + lead) // per)
 
         @pl.when(now)
         def _():
             march_prior(k)
 
-        @pl.when(k == n_windows)
-        def _():
-            for which in (B, A):
-                for i in range(5):
-                    tau[which, cols + 1 + i] = tau[which, 1 + i]
+        for q in range(n_windows - 1):
+            @pl.when((x > 0) & (k == q))
+            def _(q=q):
+                arrived(q + 1)
+
+        @pl.when(has_far & (k == n_windows))
+        def _():
+            mend(tau.at[B], TOP, ROWS)
+            tau[B, cols + 1] = tau[B, 1]
+            for i in range(1, 5):
+                tau[B, cols + 1 + i] = tau[B, 1 + i]
+
+        @pl.when(even & (k == n_windows))
+        def _():
+            mend(tau.at[A], TOP - 4, 40)
+            for i in range(5):
+                tau[A, cols + 1 + i] = tau[A, 1 + i]
 
         @pl.when(even)
         def _():
@@ -438,7 +462,7 @@
     for k in range(n_windows):
         @pl.when(has_far)
         def _(k=k):
-            each(outside(k), "wait_send")
+            each(outside(B, k, OWN), "wait_send")
             each(inner(B, k, OWN), "wait_send")
 
         @pl.when(has_next & even)
@@ -499,18 +523,17 @@
     corrected, relaxed = pl.pallas_call(
         functools.partial(kernel, cols, groups, strips),
         out_shape=(out, out),
-        in_specs=[pl.BlockSpec(memory_space=pl.ANY)] * 2,
+        in_specs=[pl.BlockSpec(memory_space=pltpu.HBM)] * 2,
         out_specs=(pl.BlockSpec(memory_space=pl.ANY),) * 2,
         scratch_shapes=[
-            frames(2, cols + 2), frames(cols), frames(2, cols + 6),
-            frames(SPAN), frames(SPAN), frames(SPAN),
+            frames(2, cols + 2), frames(cols), frames(2, cols + 6), frames(2, 7, cols + 2),
             frames(cols + 1), frames(cols + 2), frames(GROUP + 2), frames(cols), frames(cols),
             dma((2, n_windows)), dma((n_windows,)), dma((n_windows,)), dma((2 * n_windows,)),
             dma((2, 2, n_windows)), dma((2, 2, n_windows)),
             dma((n_groups,)), dma((n_groups,)), dma((n_groups,)), dma((2,)),
         ],
         compiler_params=pltpu.CompilerParams(
-            collective_id=0, has_side_effects=True, vmem_limit_bytes=61 * 2**20
+            collective_id=0, has_side_effects=True, vmem_limit_bytes=51 * 2**20
         ),
     )(start_state, guess)
     return corrected[None], relaxed[None]

time: 73.8 us -> 69.1 us (0.936)
  Pallas kernels: 69.6 us -> 66.4 us
  local copies, waits for them, and re-layouts: 3.33 us -> 1.94 us
    pallas_call x1, Pallas kernels: 69.6 us -> 66.4 us  [shards(): pl.pallas_call(functools.partial(kernel, cols, groups, strips), out_shape...]
    unnamed x4 -> x2, local copies, waits for them, and re-layouts: 3.33 us -> 1.94 us
where the time goes in v3:
time: 69.1 us; the launch traced here: 69 us
  Pallas kernels  66.4 us (96%)
  local copies, waits for them, and re-layouts  1.94 us (3%)
    pallas_call x1, Pallas kernels, shards(): pl.pallas_call(functools.partial(kernel, cols, groups, strips), out_shape...  66.4 us
    unnamed x2, local copies, waits for them, and re-layouts  1.94 us

profile of v3, /device:TPU:22, one launch (start us, length us, event | category | flops | bytes accessed | tf_op | source)
XLA Modules:
  0.0 69.0 jit_solution(16808238638042384414)
XLA Ops:
  0.6 66.4 %shard_map.41 = (f32[2,32,4096]{2,1,0:T(8,128)S(1)}, f32[2,32,4096]{2,1,0:T(8,128)S(1)}) custom-call(f32[2,32,4096]{2,1,0:T(8,128)} %start_ref.1, f32[2,32,4096]{2,1,0:T(8,128)} %bitcast.5), custom_call_target="tpu_custom_call" | custom-call | tf_op jit(solution)/shard_map/pallas_call | solution.py:523
  67.0 1.0 %copy.6 = f32[1,2,32,4096]{3,2,1,0:T(8,128)} copy(f32[1,2,32,4096]{3,2,1,0:T(8,128)S(1)} %bitcast.4) | data formatting | bytes 2097152
  68.0 1.0 %copy.7 = f32[1,2,32,4096]{3,2,1,0:T(8,128)} copy(f32[1,2,32,4096]{3,2,1,0:T(8,128)S(1)} %bitcast.3) | data formatting | bytes 2097152

commit v4 on v3

--- a/solution.py
+++ b/solution.py
@@ -441,8 +441,9 @@
 
         @pl.when(even)
         def _():
-            first = jnp.maximum(ahead * (k - 1) + 1 - x, 0)
-            stop = jnp.maximum(ahead * k + 1 - x, 0)
+            lag = jnp.maximum(x - 1, 0)
+            first = jnp.maximum(ahead * (k - 1) + 1 - lag, 0)
+            stop = jnp.maximum(ahead * k + 1 - lag, 0)
             lax.fori_loop(first, jnp.where(k == n_windows, n_groups, stop), chain, 0)
 
         return 0

time: 69.1 us -> 67.6 us (0.978)
  Pallas kernels: 66.4 us -> 64.8 us
    pallas_call x1, Pallas kernels: 66.4 us -> 64.8 us  [shards(): pl.pallas_call(functools.partial(kernel, cols, groups, strips), out_shape...]
where the time goes in v4:
time: 67.6 us; the launch traced here: 67.4 us
  Pallas kernels  64.8 us (96%)
  local copies, waits for them, and re-layouts  1.94 us (3%)
    pallas_call x1, Pallas kernels, shards(): pl.pallas_call(functools.partial(kernel, cols, groups, strips), out_shape...  64.8 us
    unnamed x2, local copies, waits for them, and re-layouts  1.94 us

profile of v4, /device:TPU:22, one launch (start us, length us, event | category | flops | bytes accessed | tf_op | source)
XLA Modules:
  0.0 67.4 jit_solution(1055375498483209629)
XLA Ops:
  0.6 64.8 %shard_map.41 = (f32[2,32,4096]{2,1,0:T(8,128)S(1)}, f32[2,32,4096]{2,1,0:T(8,128)S(1)}) custom-call(f32[2,32,4096]{2,1,0:T(8,128)} %start_ref.1, f32[2,32,4096]{2,1,0:T(8,128)} %bitcast.5), custom_call_target="tpu_custom_call" | custom-call | tf_op jit(solution)/shard_map/pallas_call | solution.py:524
  65.5 1.0 %copy.6 = f32[1,2,32,4096]{3,2,1,0:T(8,128)} copy(f32[1,2,32,4096]{3,2,1,0:T(8,128)S(1)} %bitcast.4) | data formatting | bytes 2097152
  66.5 1.0 %copy.7 = f32[1,2,32,4096]{3,2,1,0:T(8,128)} copy(f32[1,2,32,4096]{3,2,1,0:T(8,128)S(1)} %bitcast.3) | data formatting | bytes 2097152

commit v5 on v4

--- a/solution.py
+++ b/solution.py
@@ -202,13 +202,13 @@
 
         @pl.when(has_next & even)
         def _(k=k):
+            shift(k).start()
             each(onward(k, SHALLOW), "start")
+
+        @pl.when(has_next & ~even)
+        def _(k=k):
             shift(k).start()
-
-        @pl.when(has_next & ~even)
-        def _(k=k):
             each(onward(k, DEEP), "start")
-            shift(k).start()
 
     def arrived(k):
         lo, n = chunk(k)
@@ -385,7 +385,13 @@
                 mid[i, :, pl.ds(row, rows), :] = update(state, base, i, GROUP + 2, row, rows, COARSE) + tau[A, base + x + 1 + i, :, pl.ds(row, rows), :]
                 return 0
 
-            lax.fori_loop(0, GROUP + 2, rough, 0, unroll=True)
+            @pl.when(has_far)
+            def _():
+                lax.fori_loop(0, GROUP + 2, rough, 0, unroll=True)
+
+            @pl.when(~has_far)
+            def _():
+                lax.fori_loop(1, GROUP + 1, rough, 0, unroll=True)
 
             @pl.when(has_far)
             def _():

time: 67.6 us -> 66.9 us (0.990)
  Pallas kernels: 64.8 us -> 64.1 us
    pallas_call x1, Pallas kernels: 64.8 us -> 64.1 us  [shards(): pl.pallas_call(functools.partial(kernel, cols, groups, strips), out_shape...]
where the time goes in v5:
time: 66.9 us; the launch traced here: 66.7 us
  Pallas kernels  64.1 us (96%)
  local copies, waits for them, and re-layouts  1.94 us (3%)
    pallas_call x1, Pallas kernels, shards(): pl.pallas_call(functools.partial(kernel, cols, groups, strips), out_shape...  64.1 us
    unnamed x2, local copies, waits for them, and re-layouts  1.94 us

profile of v5, /device:TPU:22, one launch (start us, length us, event | category | flops | bytes accessed | tf_op | source)
XLA Modules:
  0.0 66.7 jit_solution(18000523647780814888)
XLA Ops:
  0.6 64.1 %shard_map.41 = (f32[2,32,4096]{2,1,0:T(8,128)S(1)}, f32[2,32,4096]{2,1,0:T(8,128)S(1)}) custom-call(f32[2,32,4096]{2,1,0:T(8,128)} %start_ref.1, f32[2,32,4096]{2,1,0:T(8,128)} %bitcast.5), custom_call_target="tpu_custom_call" | custom-call | tf_op jit(solution)/shard_map/pallas_call | solution.py:530
  64.7 1.0 %copy.6 = f32[1,2,32,4096]{3,2,1,0:T(8,128)} copy(f32[1,2,32,4096]{3,2,1,0:T(8,128)S(1)} %bitcast.4) | data formatting | bytes 2097152
  65.7 1.0 %copy.7 = f32[1,2,32,4096]{3,2,1,0:T(8,128)} copy(f32[1,2,32,4096]{3,2,1,0:T(8,128)S(1)} %bitcast.3) | data formatting | bytes 2097152
